TPU v7x, 128 devices: a whole 4x4x4 slice. The times are simulated.
128 devices in a mesh: dp: 4 (over y_lo, core), expert: 32 (over x, z, y_hi).
Axes of the slice: x: 4, y: 4 (y_hi: 2, y_lo: 2; y = y_hi * 2 + y_lo), z: 4, core: 2. Of those that a mesh axis runs over, the one named last changes fastest.
Arguments:
- tokens: bfloat16 [32768, 1440], P(('dp', 'expert')), may hold values from -6 to 6
- d_out: bfloat16 [32768, 1440], P(('dp', 'expert')), may hold values from -6 to 6
- route_ids: int32 [32768, 4], P(('dp', 'expert')), may hold values from 0 to 127, all different within a row; in each aligned block of 256 rows (0 to 255, 256 to 511, ...) at most 24 rows name the same one
- route_probs: float32 [32768, 4], P(('dp', 'expert')), may hold values from 0.05 to 0.5
- w_gate_up: bfloat16 [32, 1440, 2880], P('expert'), may hold values from -0.15625 to 0.15625
- gate_up_bias: float32 [32, 2880], P('expert'), may hold values from -3 to 3
- w_down: bfloat16 [32, 1440, 1440], P('expert'), may hold values from -0.15625 to 0.15625
Outputs:
- d_tokens: bfloat16 [32768, 1440], P(('dp', 'expert'))
- d_w_gate_up: bfloat16 [32, 1440, 2880], P('expert', 'dp')
- d_w_down: bfloat16 [32, 1440, 1440], P('expert', 'dp')
Inputs may be any that keep to these rules, and one draw needn't show every extreme that they name: `route_ids`: each row names 4 different experts; among the rows of one device no expert is named more than 24 times.
All inputs are finite; a program needn't handle non-finite values.
Results may differ from a plain program's by a relative error of at most 0.0059.
Values may be sent and summed in bfloat16 or wider, within the bound.
A program may use at most 192 MiB of HBM per device.

v0:
```python
import jax
import jax.numpy as jnp
from jax import lax
from jax.sharding import PartitionSpec as P


def shards(tokens, d_out, route_ids, route_probs, w_gate_up, gate_up_bias, w_down):
    owners = lax.axis_size("expert")
    tok_rows, width = tokens.shape
    top_count = route_ids.shape[1]
    hidden_units = w_down.shape[1]
    capacity = 3 * tok_rows // owners
    slot_count = owners * capacity
    route_list = route_ids.reshape(-1)
    inside = route_list < owners
    one_hot = (route_list[:, None] == jnp.arange(owners, dtype=jnp.int32)[None, :]).astype(
        jnp.int32
    )
    earlier = jnp.cumsum(one_hot, axis=0) - one_hot
    position = jnp.sum(earlier * one_hot, axis=1)
    target = jnp.where(inside, route_list * capacity + position, slot_count)
    route_rows = jnp.repeat(tokens, top_count, axis=0)
    scaled = (
        (route_probs[:, :, None] * d_out[:, None, :].astype(jnp.float32))
        .astype(jnp.bfloat16)
        .reshape(-1, width)
    )
    send_rows = jnp.zeros((slot_count, width), jnp.bfloat16).at[target].set(route_rows, mode="drop")
    send_scaled = jnp.zeros((slot_count, width), jnp.bfloat16).at[target].set(scaled, mode="drop")
    recv_rows, recv_scaled = (
        lax.all_to_all(
            send_rows.reshape(owners, capacity, width),
            "expert",
            split_axis=0,
            concat_axis=0,
            tiled=True,
        ),
        lax.all_to_all(
            send_scaled.reshape(owners, capacity, width),
            "expert",
            split_axis=0,
            concat_axis=0,
            tiled=True,
        ),
    )
    recv_rows = recv_rows.reshape(slot_count, width)
    recv_scaled = recv_scaled.reshape(slot_count, width)
    w_gu = w_gate_up[0]
    w_dn = w_down[0]
    pre = jnp.dot(recv_rows, w_gu, preferred_element_type=jnp.float32) + gate_up_bias[0][None, :]
    gate = pre[:, :hidden_units]
    upper = pre[:, hidden_units:]
    sig = jax.nn.sigmoid(1.702 * gate)
    glu = gate * sig
    hidden = ((upper + 1.0) * glu).astype(jnp.bfloat16)
    d_hidden = jnp.einsum("rd,fd->rf", recv_scaled, w_dn, preferred_element_type=jnp.float32)
    d_gate = d_hidden * (upper + 1.0) * (sig + 1.702 * gate * sig * (1.0 - sig))
    d_upper = d_hidden * glu
    d_pre = jnp.concatenate([d_gate, d_upper], axis=1).astype(jnp.bfloat16)
    d_route = jnp.einsum("rk,dk->rd", d_pre, w_gu, preferred_element_type=jnp.float32).astype(
        jnp.bfloat16
    )
    returned = lax.all_to_all(
        d_route.reshape(owners, capacity, width), "expert", split_axis=0, concat_axis=0, tiled=True
    )
    returned = returned.reshape(slot_count, width)
    fetched = returned[jnp.minimum(target, slot_count - 1)].astype(jnp.float32)
    fetched = jnp.where(inside[:, None], fetched, 0.0)
    d_tokens = jnp.sum(fetched.reshape(tok_rows, top_count, width), axis=1).astype(jnp.bfloat16)
    columns = recv_rows
    grad_gu = lax.psum_scatter(
        jnp.einsum("rd,rk->dk", columns, d_pre, preferred_element_type=jnp.float32),
        "dp",
        scatter_dimension=0,
        tiled=True,
    )
    columns = hidden
    grad_dn = lax.psum_scatter(
        jnp.einsum("rf,rd->fd", columns, recv_scaled, preferred_element_type=jnp.float32),
        "dp",
        scatter_dimension=0,
        tiled=True,
    )
    grad_gate_up = grad_gu.astype(jnp.bfloat16)[None]
    grad_down = grad_dn.astype(jnp.bfloat16)[None]
    return (d_tokens, grad_gate_up, grad_down)


def solution(mesh):
    in_specs = (
        P(("dp", "expert"), None),
        P(("dp", "expert"), None),
        P(("dp", "expert"), None),
        P(("dp", "expert"), None),
        P("expert", None, None),
        P("expert", None),
        P("expert", None, None),
    )
    out_specs = (P(("dp", "expert"), None), P("expert", "dp", None), P("expert", "dp", None))
    return jax.shard_map(shards, mesh=mesh, in_specs=in_specs, out_specs=out_specs, check_vma=False)
```

profile of v0, /device:TPU:1, one launch (start us, length us, event | category | flops | bytes accessed | tf_op | source)
XLA Modules:
  0.0 403.4 jit_solution(13128458827228416989)
XLA Ops:
  7.2 0.7 broadcast_compare_fusion
  7.9 0.7 broadcast_multiply_fusion
  8.5 0.8 copy.28
  9.4 0.1 eq.29
  9.5 0.1 eq.25
  9.6 0.2 copy.25
  9.8 0.1 lt.46
  9.9 0.1 copy.27
  10.1 0.1 mul.68
  10.2 9.0 %reduce-window.6 = s32[32,8,128]{2,1,0:T(8,128)S(1)} reduce-window(s32[32,8,128]{2,1,0:T(8,128)S(1)} %fusion.23, s32[]{:T(128)} %constant.3.clone.1), window={size=1x1x128 pad=0_0x0_0x127_0}, to_apply=%region_0.0 | reduce-window | flops 4161536 | bytes 262148 | tf_op jit(solution)/shard_map/reduce-window
  19.2 0.1 slice.18
  19.3 0.1 copy.30
  19.5 0.1 copy.31
  19.6 0.1 broadcast_add_fusion
  19.7 2.3 copy.34
  22.0 1.9 broadcast_in_dim.34
  23.9 2.9 reshape.157
  26.9 8.0 %scatter_custom_fusion.1 = bf16[768,1440]{1,0:T(8,128)(2,1)} fusion(s32[1024]{0:T(1024)S(1)} %bitcast.60, bf16[1024,1440]{1,0:T(8,128)(2,1)} %reshape.157, bf16[]{:T(256)} %constant.10.clone.1), kind=kCustom, calls=%fused_computation.27 | custom fusion | bytes 2212352 | tf_op jit(solution)/shard_map/scatter | solution.py:28
  34.9 11.8 %all-to-all-start.1 = ((bf16[32,24,1440]{2,1,0:T(8,128)(2,1)}), bf16[32,24,1440]{2,1,0:T(8,128)(2,1)}, u32[]{:S(2)}, u32[]{:S(2)}) async-start(bf16[32,24,1440]{2,1,0:T(8,128)(2,1)} %bitcast.7), calls=%async_computation.1 | async-start | bytes 4718592 | tf_op jit(solution)/shard_map/all_to_all | solution.py:31
  46.7 0.1 copy.32
  46.8 0.1 mul.70
  46.9 0.3 copy.33
  47.2 3.7 mul.72
  51.0 7.7 %mul.73 = f32[1024,1440]{1,0:T(8,128)} reshape(f32[256,4,1440]{2,1,0:T(4,128)} %mul.72) | data formatting | bytes 11796480 | tf_op jit(solution)/shard_map/mul | solution.py:24
  58.7 8.6 %scatter_custom_fusion = bf16[768,1440]{1,0:T(8,128)(2,1)} fusion(s32[1024]{0:T(1024)S(1)} %bitcast.61, f32[1024,1440]{1,0:T(8,128)} %mul.73, f32[1024]{0:T(1024)S(1)} %mul.70, bf16[]{:T(256)} %constant.10.clone.1), kind=kCustom, calls=%fused_computation.21 | custom fusion | flops 2949120 | bytes 8114178 | tf_op jit(solution)/shard_map/scatter | solution.py:29
  67.3 11.6 %all-to-all-done.1 = bf16[32,24,1440]{2,1,0:T(8,128)(2,1)} async-done(((bf16[32,24,1440]{2,1,0:T(8,128)(2,1)}), bf16[32,24,1440]{2,1,0:T(8,128)(2,1)}, u32[]{:S(2)}, u32[]{:S(2)}) %all-to-all-start.1) | async-done | bytes 2211872 | tf_op jit(solution)/shard_map/all_to_all | solution.py:31
  78.9 7.8 %all-to-all-start = ((bf16[32,24,1440]{2,1,0:T(8,128)(2,1)}), bf16[32,24,1440]{2,1,0:T(8,128)(2,1)S(1)}, u32[]{:S(2)}, u32[]{:S(2)}) async-start(bf16[32,24,1440]{2,1,0:T(8,128)(2,1)} %bitcast.4), calls=%async_computation | async-start | bytes 4718592 | tf_op jit(solution)/shard_map/all_to_all | solution.py:38
  86.7 0.6 reduce-scatter.6.cloned.1.call-start
  87.3 13.1 %fusion.4 = f32[768,2880]{0,1:T(8,128)} fusion(bf16[768,1440]{1,0:T(8,128)(2,1)} %bitcast.8, bf16[1,1440,2880]{2,1,0:T(8,128)(2,1)} %param.11, f32[2880]{0:T(1024)S(1)} %reduce), kind=kOutput, calls=%fused_computation.9 | convolution fusion | flops 6372311040 | bytes 19365120 | tf_op jit(solution)/shard_map/dot_general | solution.py:50
  100.5 18.6 %all-to-all-done = bf16[32,24,1440]{2,1,0:T(8,128)(2,1)S(1)} async-done(((bf16[32,24,1440]{2,1,0:T(8,128)(2,1)}), bf16[32,24,1440]{2,1,0:T(8,128)(2,1)S(1)}, u32[]{:S(2)}, u32[]{:S(2)}) %all-to-all-start) | async-done | bytes 2211872 | tf_op jit(solution)/shard_map/all_to_all | solution.py:38
  119.1 11.1 %fusion.15 = f32[1440,1440]{1,0:T(8,128)} fusion(bf16[768,1440]{1,0:T(8,128)(2,1)S(1)} %bitcast.54, f32[768,2880]{0,1:T(8,128)} %fusion.4), kind=kOutput, calls=%fused_computation.24 | convolution fusion | flops 3193896960 | bytes 19353600 | tf_op jit(solution)/shard_map/rf,rd->fd/dot_general | solution.py:79
  130.2 0.2 reduce-scatter.8.cloned.1.call-start
  130.4 10.3 %multiply_convert_fusion.3 = (bf16[768,1440]{0,1:T(8,128)(2,1)S(1)}, bf16[768,1440]{0,1:T(8,128)(2,1)S(1)}) fusion(f32[768,2880]{0,1:T(8,128)} %fusion.4, bf16[768,1440]{1,0:T(8,128)(2,1)S(1)} %bitcast.55, bf16[1,1440,1440]{2,1,0:T(8,128)(2,1)} %param.13), kind=kOutput, calls=%fused_computation.16 | convolution fusion | flops 3201638400 | bytes 19630080 | tf_op jit(solution)/shard_map/rd,fd->rf/dot_general | solution.py:56
  140.7 1.4 copy-done.3
  142.2 0.6 copy-done.4
  142.7 13.8 %fusion.14 = f32[1440,2880]{1,0:T(8,128)} fusion(bf16[768,1440]{1,0:T(8,128)(2,1)} %bitcast.8, bf16[768,1440]{0,1:T(8,128)(2,1)S(1)} %get-tuple-element.7, bf16[768,1440]{0,1:T(8,128)(2,1)S(1)} %get-tuple-element.6), kind=kOutput, calls=%fused_computation.23 | convolution fusion | flops 6378946560 | bytes 23224320 | tf_op jit(solution)/shard_map/rd,rk->dk/dot_general | solution.py:72
  156.6 10.9 %fusion.9 = bf16[768,1440]{0,1:T(8,128)(2,1)S(1)} fusion(bf16[1,1440,2880]{2,1,0:T(8,128)(2,1)} %param.11, bf16[768,1440]{0,1:T(8,128)(2,1)} %copy-done.4, bf16[768,1440]{0,1:T(8,128)(2,1)} %copy-done.3), kind=kOutput, calls=%fused_computation.20 | convolution fusion | flops 6380052480 | bytes 14929920 | tf_op jit(solution)/shard_map/rk,dk->rd/dot_general | solution.py:60
  167.4 2.5 copy.35
  169.9 7.7 %all-to-all-start.2 = ((bf16[32,24,1440]{2,1,0:T(8,128)(2,1)}), bf16[32,24,1440]{2,1,0:T(8,128)(2,1)S(1)}, u32[]{:S(2)}, u32[]{:S(2)}) async-start(bf16[32,24,1440]{2,1,0:T(8,128)(2,1)} %bitcast.53), calls=%async_computation.2 | async-start | bytes 4718592 | tf_op jit(solution)/shard_map/all_to_all | solution.py:63
  177.7 34.4 %all-to-all-done.2 = bf16[32,24,1440]{2,1,0:T(8,128)(2,1)S(1)} async-done(((bf16[32,24,1440]{2,1,0:T(8,128)(2,1)}), bf16[32,24,1440]{2,1,0:T(8,128)(2,1)S(1)}, u32[]{:S(2)}, u32[]{:S(2)}) %all-to-all-start.2) | async-done | bytes 2211872 | tf_op jit(solution)/shard_map/all_to_all | solution.py:63
  212.1 5.6 %gather_fusion = bf16[1024,1440]{1,0:T(8,128)(2,1)} fusion(bf16[768,1440]{1,0:T(8,128)(2,1)S(1)} %bitcast.52, s32[1024]{0:T(1024)S(1)} %broadcast_clamp_fusion), kind=kCustom, calls=%fused_computation | custom fusion | bytes 5902336 | tf_op jit(solution)/shard_map/gather | solution.py:67
  217.7 6.7 %reshape.136 = f32[256,4,1440]{2,1,0:T(4,128)} reshape(bf16[1024,1440]{1,0:T(8,128)(2,1)} %gather_fusion) | data formatting | bytes 8847360 | tf_op jit(solution)/shard_map/convert_element_type | solution.py:67
  224.4 8.0 %select_reduce_fusion = bf16[256,1440]{1,0:T(8,128)(2,1)S(1)} fusion(f32[256,4,1440]{2,1,0:T(4,128)} %reshape.136, pred[256,4]{1,0:T(8,128)(4,1)S(1)} %copy.25), kind=kLoop, calls=%fused_computation.7 | loop fusion | flops 2580480 | bytes 6636544 | tf_op jit(solution)/shard_map/reduce_sum | solution.py:69
  232.5 1.1 copy.36
  233.6 6.2 %reduce-scatter.6.cloned.1.call-done = f32[360,1440]{1,0:T(8,128)} async-done(((f32[1440,1440]{1,0:T(8,128)}), f32[360,1440]{1,0:T(8,128)}) %reduce-scatter.6.cloned.1.call-update) | async-done | bytes 2073616 | tf_op jit(solution)/shard_map/reduce_scatter | solution.py:78
  239.8 2.7 convert_bitcast_fusion.1
  242.5 150.1 %reduce-scatter.8.cloned.1.call-done = f32[360,2880]{1,0:T(8,128)} async-done(((f32[1440,2880]{1,0:T(8,128)}), f32[360,2880]{1,0:T(8,128)}) %reduce-scatter.8.cloned.1.call-update) | async-done | bytes 4147216
  392.6 3.7 convert_bitcast_fusion
  (17 shorter events, 0.2 us)
Async XLA Ops:
  26.8 19.8 %copy-start.2 = (f32[256,4]{0,1:T(4,128)S(1)}, f32[256,4]{0,1:T(4,128)}, u32[]{:S(2)}) copy-start(f32[256,4]{0,1:T(4,128)} %param.10) | copy-start | bytes 12292
  26.8 20.1 %copy-start = (bf16[256,1440]{0,1:T(8,128)(2,1)S(1)}, bf16[256,1440]{0,1:T(8,128)(2,1)}, u32[]{:S(2)}) copy-start(bf16[256,1440]{0,1:T(8,128)(2,1)} %param.8) | copy-start | bytes 2211844
  34.9 44.0 %all-to-all-start.1 = ((bf16[32,24,1440]{2,1,0:T(8,128)(2,1)}), bf16[32,24,1440]{2,1,0:T(8,128)(2,1)}, u32[]{:S(2)}, u32[]{:S(2)}) async-start(bf16[32,24,1440]{2,1,0:T(8,128)(2,1)} %bitcast.7), calls=%async_computation.1 | async-start | bytes 4718592 | tf_op jit(solution)/shard_map/all_to_all | solution.py:31
  67.3 19.9 %copy-start.1 = (f32[1,2880]{1,0:T(1,128)S(1)}, f32[1,2880]{1,0:T(1,128)}, u32[]{:S(2)}) copy-start(f32[1,2880]{1,0:T(1,128)} %param.12) | copy-start | bytes 34564
  78.9 40.2 %all-to-all-start = ((bf16[32,24,1440]{2,1,0:T(8,128)(2,1)}), bf16[32,24,1440]{2,1,0:T(8,128)(2,1)S(1)}, u32[]{:S(2)}, u32[]{:S(2)}) async-start(bf16[32,24,1440]{2,1,0:T(8,128)(2,1)} %bitcast.4), calls=%async_computation | async-start | bytes 4718592 | tf_op jit(solution)/shard_map/all_to_all | solution.py:38
  86.7 153.1 %reduce-scatter.6.cloned.1.call-start = ((), (), s32[]{:S(2)}) async-start(), calls=%async_computation.5 | async-start | bytes 11059200 | tf_op jit(solution)/shard_map/reduce_scatter | solution.py:78
  130.2 262.4 %reduce-scatter.8.cloned.1.call-start = ((), (), s32[]{:S(2)}) async-start(), calls=%async_computation.6 | async-start | bytes 21196800
  140.7 1.5 copy-start.3
  140.7 2.0 copy-start.4
  169.9 42.2 %all-to-all-start.2 = ((bf16[32,24,1440]{2,1,0:T(8,128)(2,1)}), bf16[32,24,1440]{2,1,0:T(8,128)(2,1)S(1)}, u32[]{:S(2)}, u32[]{:S(2)}) async-start(bf16[32,24,1440]{2,1,0:T(8,128)(2,1)} %bitcast.53), calls=%async_computation.2 | async-start | bytes 4718592 | tf_op jit(solution)/shard_map/all_to_all | solution.py:63
Sparse Core Ops, SparseCore 0:
  130.3 109.4 reduce-scatter.5
  242.4 150.1 reduce-scatter.7
where the time goes:
time: 409 us; the launch traced here: 403 us
  waiting for transfers between devices  221 us (54%)
  matrix products  59.2 us (14%)
  local copies, waits for them, and re-layouts  47 us (11%)
  other arithmetic  33.8 us (8%)
  starting transfers between devices  28.1 us (7%)
  between operations  14.5 us (4%)
    unnamed x3, waiting for transfers between devices  150 us
    all_to_all x1, waiting for transfers between devices, shards(): lax.all_to_all(d_route.reshape(owners, capacity, width), 'expert', split_...  34.4 us
    all_to_all x1, waiting for transfers between devices, shards(): lax.all_to_all(send_scaled.reshape(owners, capacity, width), 'expert', sp...  18.6 us
    dot_general x1, matrix products, shards(): jnp.einsum('rd,rk->dk', columns, d_pre, preferred_element_type=jnp.float32)  13.8 us
    dot_general x1, matrix products, shards(): jnp.dot(recv_rows, w_gu, preferred_element_type=jnp.float32)  13.1 us
    all_to_all x1, starting transfers between devices, shards(): lax.all_to_all(send_rows.reshape(owners, capacity, width), 'expert', spli...  11.8 us
    mul x3, local copies, waits for them, and re-layouts, shards(): route_probs[:, :, None] * d_out[:, None, :].astype(jnp.float32)  11.6 us
    all_to_all x1, waiting for transfers between devices, shards(): lax.all_to_all(send_rows.reshape(owners, capacity, width), 'expert', spli...  11.6 us
  transfers between devices with their start and end apart: 5, of which 5 were waited for; matrix products, arithmetic and copies ran while one was open for 24% of the time, Pallas kernels for 0%

commit v1 on v0

v1 whole, which is shorter than its diff:
```python
import jax
import jax.numpy as jnp
from jax import lax
from jax.experimental import pallas as pl
from jax.experimental.pallas import tpu as pltpu
from jax.sharding import PartitionSpec as P

MESH = pl.DeviceIdType.MESH
F32 = jnp.float32
BF16 = jnp.bfloat16
OWNERS = 32
CAP = 24
WIDTH = 1440
HALF = 720
SHARD = 360
PAD = 1536
TILE = 512
GROUP = 8
ROWS = GROUP * CAP


def nt(a, b):
    return lax.dot_general(a, b, (((1,), (1,)), ((), ())), preferred_element_type=F32)


def tn(a, b):
    return lax.dot_general(a, b, (((0,), (0,)), ((), ())), preferred_element_type=F32)


def nn(a, b):
    return jnp.dot(a, b, preferred_element_type=F32)


def route_kernel(ids_ref, probs_ref, tok_ref, dout_ref, rows_ref, scaled_ref, pick_ref):
    me = lax.axis_index("expert")
    toks = ids_ref.shape[1]
    r = lax.broadcasted_iota(jnp.int32, (OWNERS, toks), 0)
    i = (r >> 1) & 3
    x = ((me >> 3) + i) & 3
    z = ((me >> 1) + (r >> 3) - i) & 3
    expert = x * 8 + z * 2 + ((me ^ r) & 1)
    named = jnp.zeros((OWNERS, toks), F32)
    prob = jnp.zeros((OWNERS, toks), F32)
    for k in range(ids_ref.shape[0]):
        hit = ids_ref[k : k + 1, :] == expert
        named = named + jnp.where(hit, 1.0, 0.0)
        prob = prob + jnp.where(hit, probs_ref[k : k + 1, :], 0.0)
    before = lax.broadcasted_iota(jnp.int32, (toks, toks), 0) < lax.broadcasted_iota(
        jnp.int32, (toks, toks), 1
    )
    rank = nn(named.astype(BF16), jnp.where(before, 1.0, 0.0).astype(BF16))
    code = jnp.where(named > 0.0, rank, -1.0)
    step = 8
    for g in range(OWNERS // step):
        part = slice(step * g, step * g + step)
        lines = slice(step * CAP * g, step * CAP * (g + 1))
        place = lax.broadcasted_iota(jnp.int32, (step, CAP, toks), 1).astype(F32)
        pick = jnp.broadcast_to(code[part][:, None, :], (step, CAP, toks)) == place
        pick = pick.reshape(step * CAP, toks) if False else pick
        ones = jnp.where(pick, 1.0, 0.0)
        weight = jnp.sum(
            jnp.where(pick, jnp.broadcast_to(prob[part][:, None, :], (step, CAP, toks)), 0.0),
            axis=2,
            keepdims=True,
        ).reshape(step * CAP, 1)
        ones = ones.reshape(step * CAP, toks).astype(BF16)
        pick_ref[lines, :] = ones
        rows_ref[lines, :] = nn(ones, tok_ref[...]).astype(BF16)
        scaled_ref[lines, :] = (nn(ones, dout_ref[...]) * weight).astype(BF16)


def combine_kernel(pick_ref, back_ref, out_ref):
    out_ref[...] = tn(pick_ref[...], back_ref[...]).astype(BF16)


def main_kernel(
    bias_ref,
    rows_ref,
    scaled_ref,
    wgu_ref,
    wdn_ref,
    out_gu_ref,
    out_dn_ref,
    back_ref,
    got_rows,
    got_scaled,
    wgu,
    wu,
    wdn,
    acc,
    dgate,
    dup,
    hid,
    rows_t,
    hid_t,
    droute,
    give,
    take,
    w_sem,
    send_sem,
    recv_sem,
    fwd_send,
    fwd_recv,
    back_send,
    back_recv,
    self_sem,
    core_send,
    core_recv,
):
    dp = lax.axis_index("dp")
    me = lax.axis_index("expert")
    l = dp // 2
    c = dp % 2
    mx, mz, mh = me // 8, (me // 2) % 4, me % 2

    def target(r, sign):
        k, i, low = r // 8, (r // 2) % 4, r % 2
        x = (mx + sign * i + 4) % 4
        z = (mz + sign * (k - i) + 8) % 4
        h = (mh + low) % 2
        return (((l + low) % 2) * 2 + c, x * 8 + z * 2 + h)

    over_y = ((1 - l) * 2 + c, me)
    over_core = (l * 2 + 1 - c, me)

    load_gu = pltpu.make_async_copy(wgu_ref.at[0], wgu, w_sem.at[0])
    load_dn = pltpu.make_async_copy(wdn_ref.at[0], wdn.at[pl.ds(0, WIDTH)], w_sem.at[1])
    load_gu.start()
    load_dn.start()

    barrier = pltpu.get_barrier_semaphore()

    def greet(r, _):
        pl.semaphore_signal(barrier, inc=1, device_id=target(r, 1), device_id_type=MESH)
        return 0

    lax.fori_loop(1, OWNERS, greet, 0)
    pl.semaphore_signal(barrier, inc=1, device_id=over_y, device_id_type=MESH)
    pl.semaphore_signal(barrier, inc=1, device_id=over_core, device_id_type=MESH)
    pl.semaphore_wait(barrier, OWNERS + 1)

    def slot(ref, region, r):
        return ref.at[region, r // 4, r % 4]

    for n, (src, dst) in enumerate(((rows_ref, got_rows), (scaled_ref, got_scaled))):
        pltpu.make_async_copy(src.at[0], dst.at[0, 0, 0], recv_sem.at[0, n]).start()

    def dispatch(r, _):
        for n, (src, dst) in enumerate(((rows_ref, got_rows), (scaled_ref, got_scaled))):
            pltpu.make_async_remote_copy(
                src_ref=src.at[r],
                dst_ref=slot(dst, 0, r),
                send_sem=send_sem.at[n],
                recv_sem=recv_sem.at[r // 4, n],
                device_id=target(r, 1),
                device_id_type=MESH,
            ).start()
        return 0

    lax.fori_loop(1, OWNERS, dispatch, 0)

    def forward(p, n):
        buf = (got_rows, got_scaled)[n]
        return pltpu.make_async_remote_copy(
            src_ref=buf.at[0, p],
            dst_ref=buf.at[1, p],
            send_sem=fwd_send.at[p, n],
            recv_sem=fwd_recv.at[p, n],
            device_id=over_y,
            device_id_type=MESH,
        )

    def relay(p, _):
        for n, buf in enumerate((got_rows, got_scaled)):
            pltpu.make_async_copy(buf.at[0, p], buf.at[0, p], recv_sem.at[p, n]).wait()
            forward(p, n).start()
        return 0

    lax.fori_loop(0, 2, relay, 0)

    load_gu.wait()
    load_dn.wait()
    wdn[WIDTH:PAD, :] = jnp.zeros((PAD - WIDTH, WIDTH), BF16)
    wu[:, WIDTH:PAD] = jnp.zeros((WIDTH, PAD - WIDTH), BF16)

    def shift(q, _):
        lines = pl.ds(pl.multiple_of(q * 144, 16), 144)
        wu[lines, 0:WIDTH] = wgu[lines, WIDTH : 2 * WIDTH]
        return 0

    lax.fori_loop(0, 10, shift, 0)
    acc[...] = jnp.zeros_like(acc)

    def inner(region, j):
        lines = slice(region * ROWS, (region + 1) * ROWS)
        x = got_rows[region, pl.ds(2 * j, 2)].reshape(ROWS, WIDTH)
        y = got_scaled[region, pl.ds(2 * j, 2)].reshape(ROWS, WIDTH)
        for t in range(PAD // TILE):
            cols = slice(t * TILE, (t + 1) * TILE)
            bias_u = bias_ref[:, WIDTH + t * TILE : min(WIDTH + (t + 1) * TILE, 2 * WIDTH)]
            if bias_u.shape[1] < TILE:
                bias_u = jnp.concatenate(
                    [bias_u, jnp.zeros((1, TILE - bias_u.shape[1]), F32)], axis=1
                )
            g = nn(x, wgu[:, cols]) + bias_ref[:, cols]
            u = nn(x, wu[:, cols]) + bias_u + 1.0
            dh = nt(y, wdn[cols, :])
            s = jax.nn.sigmoid(1.702 * g)
            glu = g * s
            hid[lines, cols] = (u * glu).astype(BF16)
            dup[lines, cols] = (dh * glu).astype(BF16)
            dgate[lines, cols] = (dh * u * (s + 1.702 * glu * (1.0 - s))).astype(BF16)

    def back_copy(r):
        return pltpu.make_async_remote_copy(
            src_ref=droute.at[r],
            dst_ref=back_ref.at[r],
            send_sem=back_send,
            recv_sem=back_recv,
            device_id=target(r, -1),
            device_id_type=MESH,
        )

    own_back = pltpu.make_async_copy(droute.at[0], back_ref.at[0], self_sem)

    def superstep(j, _):
        @pl.when(j < 3)
        def _():
            lax.fori_loop(2 * j + 2, 2 * j + 4, relay, 0)

        inner(0, j)
        for first in range(0, WIDTH, TILE):
            cols = slice(first, min(first + TILE, WIDTH))
            part = nt(dgate[0:ROWS, :], wgu[cols, 0:PAD]) + nt(dup[0:ROWS, :], wu[cols, :])
            part = part.reshape(GROUP, CAP, cols.stop - cols.start).astype(BF16)
            droute[pl.ds(GROUP * j, GROUP), :, cols] = part

        def send_back(r, _):
            @pl.when(r == 0)
            def _():
                own_back.start()

            @pl.when(r > 0)
            def _():
                back_copy(r).start()

            return 0

        lax.fori_loop(GROUP * j, GROUP * j + GROUP, send_back, 0)

        def arrive(p, _):
            for n in range(2):
                forward(p, n).wait_recv()
            return 0

        lax.fori_loop(2 * j, 2 * j + 2, arrive, 0)
        inner(1, j)
        x = got_rows[:, pl.ds(2 * j, 2)].reshape(2 * ROWS, WIDTH)
        y = got_scaled[:, pl.ds(2 * j, 2)].reshape(2 * ROWS, WIDTH)
        for side in range(2):

            @pl.when(l == side)
            def _():
                cols = slice(HALF * side, HALF * (side + 1))
                rows_t[...] = x[:, cols].T
                hid_t[...] = hid[:, cols].T

        for t in range(PAD // TILE):
            cols = slice(t * TILE, (t + 1) * TILE)
            acc[0, :, cols] += nn(rows_t[...], dgate[:, cols])
            acc[1, :, cols] += nn(rows_t[...], dup[:, cols])
            cols = slice(t * TILE, min((t + 1) * TILE, WIDTH))
            acc[2, :, cols] += nn(hid_t[...], y[:, cols])
        return 0

    lax.fori_loop(0, 4, superstep, 0)

    def core_copy(n):
        return pltpu.make_async_remote_copy(
            src_ref=give.at[n],
            dst_ref=take.at[n],
            send_sem=core_send.at[n],
            recv_sem=core_recv.at[n],
            device_id=over_core,
            device_id_type=MESH,
        )

    other = pl.ds(pl.multiple_of((1 - c) * SHARD, 8), SHARD)
    mine = pl.ds(pl.multiple_of(c * SHARD, 8), SHARD)
    for n in range(3):
        give[n] = acc[n, other, 0:WIDTH].astype(BF16)
        core_copy(n).start()
    outs = (out_gu_ref.at[:, 0:WIDTH], out_gu_ref.at[:, WIDTH : 2 * WIDTH], out_dn_ref)
    for n in range(3):
        core_copy(n).wait_recv()
        total = (acc[n, mine, 0:WIDTH] + take[n].astype(F32)).astype(BF16)
        if n == 0:
            out_gu_ref[:, 0:WIDTH] = total
        elif n == 1:
            out_gu_ref[:, WIDTH : 2 * WIDTH] = total
        else:
            out_dn_ref[...] = total

    for n in range(3):
        core_copy(n).wait_send()
    for n, src in enumerate((rows_ref, scaled_ref)):
        some = src.at[pl.ds(1, OWNERS - 1)]
        pltpu.make_async_copy(some, some, send_sem.at[n]).wait()

    def settle(p, _):
        for n in range(2):
            forward(p, n).wait_send()
        return 0

    lax.fori_loop(0, 8, settle, 0)
    some = droute.at[pl.ds(1, OWNERS - 1)]
    pltpu.make_async_copy(some, some, back_send).wait()
    some = back_ref.at[pl.ds(1, OWNERS - 1)]
    pltpu.make_async_copy(some, some, back_recv).wait()
    own_back.wait()


def shards(tokens, d_out, route_ids, route_probs, w_gate_up, gate_up_bias, w_down):
    toks = tokens.shape[0]
    vmem = pl.BlockSpec(memory_space=pltpu.VMEM)
    hbm = pl.BlockSpec(memory_space=pl.ANY)
    slots = OWNERS * CAP
    rows, scaled, pick = pl.pallas_call(
        route_kernel,
        name="route",
        out_shape=(
            jax.ShapeDtypeStruct((slots, WIDTH), BF16),
            jax.ShapeDtypeStruct((slots, WIDTH), BF16),
            jax.ShapeDtypeStruct((slots, toks), BF16),
        ),
        in_specs=[vmem] * 4,
        out_specs=(vmem, vmem, vmem),
        compiler_params=pltpu.CompilerParams(vmem_limit_bytes=40 * 2**20),
    )(route_ids.T, route_probs.T, tokens, d_out)
    blocks = (OWNERS, CAP, WIDTH)
    grad_gu, grad_dn, back = pl.pallas_call(
        main_kernel,
        name="experts",
        out_shape=(
            jax.ShapeDtypeStruct((SHARD, 2 * WIDTH), BF16),
            jax.ShapeDtypeStruct((SHARD, WIDTH), BF16),
            jax.ShapeDtypeStruct(blocks, BF16),
        ),
        in_specs=[vmem, hbm, hbm, hbm, hbm],
        out_specs=(vmem, vmem, hbm),
        scratch_shapes=[
            pltpu.VMEM((2, 8, 4, CAP, WIDTH), BF16),
            pltpu.VMEM((2, 8, 4, CAP, WIDTH), BF16),
            pltpu.VMEM((WIDTH, 2 * WIDTH), BF16),
            pltpu.VMEM((WIDTH, PAD), BF16),
            pltpu.VMEM((PAD, WIDTH), BF16),
            pltpu.VMEM((3, HALF, PAD), F32),
            pltpu.VMEM((2 * ROWS, PAD), BF16),
            pltpu.VMEM((2 * ROWS, PAD), BF16),
            pltpu.VMEM((2 * ROWS, PAD), BF16),
            pltpu.VMEM((HALF, 2 * ROWS), BF16),
            pltpu.VMEM((HALF, 2 * ROWS), BF16),
            pltpu.VMEM(blocks, BF16),
            pltpu.VMEM((3, SHARD, WIDTH), BF16),
            pltpu.VMEM((3, SHARD, WIDTH), BF16),
            pltpu.SemaphoreType.DMA((2,)),
            pltpu.SemaphoreType.DMA((2,)),
            pltpu.SemaphoreType.DMA((8, 2)),
            pltpu.SemaphoreType.DMA((8, 2)),
            pltpu.SemaphoreType.DMA((8, 2)),
            pltpu.SemaphoreType.DMA,
            pltpu.SemaphoreType.DMA,
            pltpu.SemaphoreType.DMA,
            pltpu.SemaphoreType.DMA((3,)),
            pltpu.SemaphoreType.DMA((3,)),
        ],
        compiler_params=pltpu.CompilerParams(
            collective_id=0, has_side_effects=True, vmem_limit_bytes=63 * 2**20
        ),
    )(gate_up_bias, rows.reshape(blocks), scaled.reshape(blocks), w_gate_up, w_down)
    d_tokens = pl.pallas_call(
        combine_kernel,
        name="combine",
        out_shape=jax.ShapeDtypeStruct((toks, WIDTH), BF16),
        in_specs=[vmem, vmem],
        out_specs=vmem,
        compiler_params=pltpu.CompilerParams(vmem_limit_bytes=40 * 2**20),
    )(pick, back.reshape(slots, WIDTH))
    return d_tokens, grad_gu[None], grad_dn[None]


def solution(mesh):
    in_specs = (
        P(("dp", "expert"), None),
        P(("dp", "expert"), None),
        P(("dp", "expert"), None),
        P(("dp", "expert"), None),
        P("expert", None, None),
        P("expert", None),
        P("expert", None, None),
    )
    out_specs = (P(("dp", "expert"), None), P("expert", "dp", None), P("expert", "dp", None))
    return jax.shard_map(shards, mesh=mesh, in_specs=in_specs, out_specs=out_specs, check_vma=False)
```

time: 409 us -> 155 us (0.38)
  the two profiles are of different devices: /device:TPU:1 before, /device:TPU:13 now
where the time goes in v1:
time: 155 us
  Pallas kernels  141 us (91%)
  local copies, waits for them, and re-layouts  12.6 us (8%)
    pallas_call x1, Pallas kernels, shards(): pl.pallas_call(main_kernel, name='experts', out_shape=(jax.ShapeDtypeStru...  139 us
    unnamed x17, local copies, waits for them, and re-layouts  12.6 us

profile of v1, /device:TPU:13, one launch (start us, length us, event | category | flops | bytes accessed | tf_op | source)
XLA Modules:
  0.0 154.8 jit_solution(14744433243363010341)
XLA Ops:
  0.6 0.0 copy-start.4
  0.6 0.0 copy-start.3
  0.7 1.4 copy.10.tok_ref
  2.1 1.4 copy.11.dout_ref
  3.5 0.0 copy-done.4
  3.5 0.0 copy-done.3
  3.5 1.6 %route.1 = (bf16[768,1440]{1,0:T(8,128)(2,1)S(1)}, bf16[768,1440]{1,0:T(8,128)(2,1)S(1)}, bf16[768,256]{1,0:T(8,128)(2,1)S(1)}) custom-call(s32[4,256]{1,0:T(4,128)S(1)} %bitcast.10, f32[4,256]{1,0:T(4,128)S(1)} %bitcast.11, bf16[256,1440]{1,0:T(8,128)(2,1)S(1)} %copy.10.tok_ref, bf16[256,1440]{1,0:T(8,128)(2,1)S(1)} %copy.11.dout_ref), custom_call_target="tpu_custom_call" | custom-call | tf_op jit(solution)/shard_map/route/pallas_call | solution.py:328
  5.1 0.0 copy-start.1
  5.1 1.4 copy-done.1
  6.5 0.0 copy-start.2
  6.5 1.4 copy-done.2
  7.9 139.1 %experts.1 = (bf16[360,2880]{1,0:T(8,128)(2,1)}, bf16[360,1440]{1,0:T(8,128)(2,1)}, bf16[32,24,1440]{2,1,0:T(8,128)(2,1)}) custom-call(f32[1,2880]{1,0:T(1,128)} %bias_ref.1, bf16[32,24,1440]{2,1,0:T(8,128)(2,1)} %bitcast.8, bf16[32,24,1440]{2,1,0:T(8,128)(2,1)} %bitcast.9, bf16[1,1440,2880]{2,1,0:T(8,128)(2,1)} %wgu_ref.1, bf16[1,1440,1440]{2,1,0:T(8,128)(2,1)} %wdn_ref.1), custom_call_target="tpu_custom_call" | custom-call | tf_op jit(solution)/shard_map/experts/pallas_call | solution.py:341
  147.0 0.0 copy-start
  147.0 1.7 %copy-done = bf16[32,24,1440]{2,1,0:T(8,128)(2,1)S(1)} copy-done((bf16[32,24,1440]{2,1,0:T(8,128)(2,1)S(1)}, bf16[32,24,1440]{2,1,0:T(8,128)(2,1)}, u32[]{:S(2)}) %copy-start) | copy-done | bytes 2211864
  148.7 0.8 combine.1
  149.5 1.1 copy.12
  150.6 0.0 copy-start.5
  150.6 3.2 %copy.15 = bf16[1,360,2880]{2,1,0:T(8,128)(2,1)} copy(bf16[1,360,2880]{2,1,0:T(8,128)(2,1)} %bitcast.12) | data formatting | bytes 4147200
  153.8 0.0 copy-done.5
  153.8 1.0 copy.16
Async XLA Ops:
  0.6 2.8 %copy-start.4 = (f32[256,4]{0,1:T(4,128)S(1)}, f32[256,4]{0,1:T(4,128)}, u32[]{:S(2)}) copy-start(f32[256,4]{0,1:T(4,128)} %param.10) | copy-start | bytes 12292
  0.6 2.8 %copy-start.3 = (s32[256,4]{0,1:T(4,128)S(1)}, s32[256,4]{0,1:T(4,128)}, u32[]{:S(2)}) copy-start(s32[256,4]{0,1:T(4,128)} %param.9) | copy-start | bytes 12292
  5.1 1.4 copy-start.1
  6.5 1.4 copy-start.2
  147.0 1.7 %copy-start = (bf16[32,24,1440]{2,1,0:T(8,128)(2,1)S(1)}, bf16[32,24,1440]{2,1,0:T(8,128)(2,1)}, u32[]{:S(2)}) copy-start(bf16[32,24,1440]{2,1,0:T(8,128)(2,1)} %get-tuple-element.12) | copy-start | bytes 6635524
  150.6 3.2 %copy-start.5 = (bf16[360,1440]{1,0:T(8,128)(2,1)S(1)}, bf16[360,1440]{1,0:T(8,128)(2,1)}, u32[]{:S(2)}) copy-start(bf16[360,1440]{1,0:T(8,128)(2,1)} %get-tuple-element.14) | copy-start | bytes 3110404

commit v2 on v1

v2 whole, which is shorter than its diff:
```python
import jax
import jax.numpy as jnp
from jax import lax
from jax.experimental import pallas as pl
from jax.experimental.pallas import tpu as pltpu
from jax.sharding import PartitionSpec as P

MESH = pl.DeviceIdType.MESH
F32 = jnp.float32
BF16 = jnp.bfloat16
OWNERS = 32
CAP = 24
WIDTH = 1440
MAIN = 1408
HALF = 720
SHARD = 360
LINES = 368
PAD = 1536
TILE = 512
GROUP = 8
ROWS = GROUP * CAP


def nt(a, b):
    return lax.dot_general(a, b, (((1,), (1,)), ((), ())), preferred_element_type=F32)


def tn(a, b):
    return lax.dot_general(a, b, (((0,), (0,)), ((), ())), preferred_element_type=F32)


def nn(a, b):
    return jnp.dot(a, b, preferred_element_type=F32)


def finish_kernel(
    pick_ref, back_ref, gu_ref, dn_ref, tok_ref, out_gu_ref, out_dn_ref, pick, back, gu, dn, sem
):
    ins = [
        pltpu.make_async_copy(src, dst, sem.at[n])
        for n, (src, dst) in enumerate(
            ((back_ref, back), (pick_ref, pick), (dn_ref, dn), (gu_ref, gu))
        )
    ]
    outs = [
        pltpu.make_async_copy(dn, out_dn_ref, sem.at[4]),
        pltpu.make_async_copy(gu, out_gu_ref, sem.at[5]),
    ]
    for copy in ins:
        copy.start()
    for n in range(2):
        ins[2 + n].wait()
        outs[n].start()
    ins[0].wait()
    ins[1].wait()
    tok_ref[...] = tn(pick[...], back[:, 0:WIDTH]).astype(BF16).T
    for copy in outs:
        copy.wait()


def main_kernel(
    ids_ref,
    probs_ref,
    bias_ref,
    tok_ref,
    dout_ref,
    wgu_ref,
    wdn_ref,
    pick_ref,
    out_gu_ref,
    out_dn_ref,
    back_ref,
    tok,
    dout,
    code,
    prob,
    send,
    got,
    rows,
    scaled,
    wgu,
    wu,
    wdn,
    acc,
    work,
    rows_t,
    hid_t,
    take,
    load_sem,
    send_sem,
    recv_sem,
    fwd_send,
    fwd_recv,
    back_send,
    back_recv,
    self_sem,
    core_send,
    core_recv,
):
    dp = lax.axis_index("dp")
    me = lax.axis_index("expert")
    l = dp // 2
    c = dp % 2
    mx, mz, mh = me // 8, (me // 2) % 4, me % 2

    def target(r, sign):
        k, i, low = r // 8, (r // 2) % 4, r % 2
        x = (mx + sign * i + 4) % 4
        z = (mz + sign * (k - i) + 8) % 4
        h = (mh + low) % 2
        return (((l + low) % 2) * 2 + c, x * 8 + z * 2 + h)

    over_y = ((1 - l) * 2 + c, me)
    over_core = (l * 2 + 1 - c, me)

    loads = [
        pltpu.make_async_copy(src, dst, load_sem.at[n])
        for n, (src, dst) in enumerate(
            (
                (tok_ref, tok),
                (dout_ref, dout),
                (wgu_ref.at[0], wgu),
                (wdn_ref.at[0], wdn.at[pl.ds(0, WIDTH)]),
            )
        )
    ]
    for load in loads[:2]:
        load.start()

    barrier = pltpu.get_barrier_semaphore()

    def greet(r, _):
        pl.semaphore_signal(barrier, inc=1, device_id=target(r, 1), device_id_type=MESH)
        return 0

    lax.fori_loop(1, OWNERS, greet, 0)
    pl.semaphore_signal(barrier, inc=1, device_id=over_y, device_id_type=MESH)
    pl.semaphore_signal(barrier, inc=1, device_id=over_core, device_id_type=MESH)

    toks = ids_ref.shape[1]
    r = lax.broadcasted_iota(jnp.int32, (OWNERS, toks), 0)
    i = (r >> 1) & 3
    x = ((me >> 3) + i) & 3
    z = ((me >> 1) + (r >> 3) - i) & 3
    expert = x * 8 + z * 2 + ((me ^ r) & 1)
    named = jnp.zeros((OWNERS, toks), F32)
    weight = jnp.zeros((OWNERS, toks), F32)
    for k in range(ids_ref.shape[0]):
        hit = ids_ref[k : k + 1, :] == expert
        named = named + jnp.where(hit, 1.0, 0.0)
        weight = weight + jnp.where(hit, probs_ref[k : k + 1, :], 0.0)
    before = lax.broadcasted_iota(jnp.int32, (toks, toks), 0) < lax.broadcasted_iota(
        jnp.int32, (toks, toks), 1
    )
    rank = nn(named.astype(BF16), jnp.where(before, 1.0, 0.0).astype(BF16))
    code[...] = jnp.where(named > 0.0, rank, -1.0)
    prob[...] = weight
    for load in loads[:2]:
        load.wait()
    for load in loads[2:]:
        load.start()

    def fill(g):
        part = pl.ds(pl.multiple_of(g * GROUP, GROUP), GROUP)
        place = lax.broadcasted_iota(jnp.int32, (GROUP, CAP, toks), 1).astype(F32)
        chosen = jnp.broadcast_to(code[part, :][:, None, :], place.shape) == place
        ones = jnp.where(chosen, 1.0, 0.0).reshape(ROWS, toks).astype(BF16)
        share = jnp.where(chosen, jnp.broadcast_to(prob[part, :][:, None, :], place.shape), 0.0)
        share = jnp.sum(share, axis=2, keepdims=True).reshape(ROWS, 1)
        pick_ref[pl.ds(pl.multiple_of(g * ROWS, ROWS), ROWS), :] = ones
        both = pl.ds(2 * g, 2)
        for n, src in enumerate((tok, dout)):
            value = nt(ones, src[...])
            if n == 1:
                value = value * share
            for first, last, where in (
                (0, MAIN, n * MAIN),
                (MAIN, WIDTH, 2 * MAIN + n * (WIDTH - MAIN)),
            ):
                piece = value[:, first:last].reshape(2, GROUP // 2, CAP, last - first)
                send[both, :, :, where : where + last - first] = piece.astype(BF16)

    def slot(region, r):
        return got.at[region, r // 4, r % 4]

    def relay_copy(src, dst, r, device):
        return pltpu.make_async_remote_copy(
            src_ref=src,
            dst_ref=dst,
            send_sem=fwd_send.at[r],
            recv_sem=fwd_recv.at[r],
            device_id=device,
            device_id_type=MESH,
        )

    def forward_block(r):
        return relay_copy(slot(0, r), slot(1, r), r, over_y)

    def dispatch(r, _):
        pltpu.make_async_remote_copy(
            src_ref=send.at[r // 4, r % 4],
            dst_ref=slot(0, r),
            send_sem=send_sem.at[r // 4],
            recv_sem=recv_sem.at[r],
            device_id=target(r, 1),
            device_id_type=MESH,
        ).start()
        return 0

    fill(0)
    pl.semaphore_wait(barrier, OWNERS + 1)
    own = pltpu.make_async_copy(send.at[0, 0], slot(0, 0), recv_sem.at[0])
    own.start()
    relay_copy(send.at[0, 0], slot(1, 0), 0, over_y).start()
    lax.fori_loop(1, GROUP, dispatch, 0)

    def fill_next(g, _):
        fill(g)
        lax.fori_loop(GROUP * g, GROUP * g + GROUP, dispatch, 0)
        return 0

    lax.fori_loop(1, OWNERS // GROUP, fill_next, 0)

    loads[2].wait()
    loads[3].wait()
    wdn[WIDTH:PAD, :] = jnp.zeros((PAD - WIDTH, WIDTH), BF16)
    wu[:, WIDTH:PAD] = jnp.zeros((WIDTH, PAD - WIDTH), BF16)

    def shift(q, _):
        lines = pl.ds(pl.multiple_of(q * 144, 16), 144)
        wu[lines, 0:WIDTH] = wgu[lines, WIDTH : 2 * WIDTH]
        return 0

    lax.fori_loop(0, 10, shift, 0)
    own.wait()

    def landed(r):
        pltpu.make_async_copy(slot(0, r), slot(0, r), recv_sem.at[r]).wait()

    def relay_block(r, _):
        landed(r)
        forward_block(r).start()
        return 0

    lax.fori_loop(1, GROUP, relay_block, 0)
    acc[...] = jnp.zeros_like(acc)

    def inner(region, j):
        lines = slice(region * ROWS, (region + 1) * ROWS)
        both = pl.ds(2 * j, 2)
        tail = 2 * MAIN
        more = WIDTH - MAIN
        for n, dst in enumerate((rows, scaled)):
            dst[lines, 0:MAIN] = got[region, both, :, :, n * MAIN : (n + 1) * MAIN].reshape(
                ROWS, MAIN
            )
        ends = got[region, both, :, :, tail : tail + 2 * more].reshape(ROWS, 2 * more)
        rows[lines, MAIN:WIDTH] = ends[:, 0:more]
        scaled[lines, MAIN:WIDTH] = ends[:, more:]
        for t in range(PAD // TILE):
            cols = slice(t * TILE, (t + 1) * TILE)
            bias_u = bias_ref[:, WIDTH + t * TILE : min(WIDTH + (t + 1) * TILE, 2 * WIDTH)]
            if bias_u.shape[1] < TILE:
                bias_u = jnp.concatenate(
                    [bias_u, jnp.zeros((1, TILE - bias_u.shape[1]), F32)], axis=1
                )
            g = nn(rows[lines, :], wgu[:, cols]) + bias_ref[:, cols]
            u = nn(rows[lines, :], wu[:, cols]) + bias_u + 1.0
            dh = nt(scaled[lines, :], wdn[cols, :])
            s = jax.nn.sigmoid(1.702 * g)
            glu = g * s
            work[2, lines, cols] = (u * glu).astype(BF16)
            work[1, lines, cols] = (dh * glu).astype(BF16)
            work[0, lines, cols] = (dh * u * (s + 1.702 * glu * (1.0 - s))).astype(BF16)

    def sent(p, count):
        some = send.at[p, pl.ds(4 - count, count)]
        pltpu.make_async_copy(some, some, send_sem.at[p]).wait()

    def back_copy(r):
        return pltpu.make_async_remote_copy(
            src_ref=send.at[r // 4, r % 4, :, pl.ds(0, PAD)],
            dst_ref=back_ref.at[r],
            send_sem=back_send,
            recv_sem=back_recv,
            device_id=target(r, -1),
            device_id_type=MESH,
        )

    own_back = pltpu.make_async_copy(
        send.at[0, 0, :, pl.ds(0, PAD)], back_ref.at[0], self_sem
    )

    def give_back(j):
        @pl.when(j == 0)
        def _():
            sent(0, 3)
            sent(1, 4)
            forward_block(0).wait_send()

        @pl.when(j > 0)
        def _():
            sent(2 * j, 4)
            sent(2 * j + 1, 4)

        for first in range(0, WIDTH, TILE):
            cols = slice(first, min(first + TILE, WIDTH))
            part = nt(work[0, 0:ROWS, :], wgu[cols, 0:PAD]) + nt(work[1, 0:ROWS, :], wu[cols, :])
            part = part.reshape(2, GROUP // 2, CAP, cols.stop - cols.start).astype(BF16)
            send[pl.ds(2 * j, 2), :, :, cols] = part

        def send_back(r, _):
            @pl.when(r == 0)
            def _():
                own_back.start()

            @pl.when(r > 0)
            def _():
                back_copy(r).start()

            return 0

        lax.fori_loop(GROUP * j, GROUP * j + GROUP, send_back, 0)

    def arrive(j):
        def one(r, _):
            forward_block(r).wait_recv()
            return 0

        lax.fori_loop(GROUP * j, GROUP * j + GROUP, one, 0)

    def turn(lines):
        at = slice(0, lines.stop - lines.start)
        for side in range(2):

            @pl.when(l == side)
            def _():
                cols = slice(HALF * side, HALF * (side + 1))
                rows_t[:, at] = rows[lines, cols].T
                hid_t[:, at] = work[2, lines, cols].T

    def add(n, lines):
        left = (rows_t, rows_t, hid_t)[n].at[:, 0 : lines.stop - lines.start]
        for t in range(PAD // TILE):
            cols = slice(t * TILE, (t + 1) * TILE)
            if n < 2:
                acc[n, :, cols] += nn(left[...], work[n, lines, cols])
            else:
                cols = slice(t * TILE, min((t + 1) * TILE, WIDTH))
                acc[n, :, cols] += nn(left[...], scaled[lines, cols])

    every = slice(0, 2 * ROWS)

    def superstep(j, _):
        lax.fori_loop(GROUP * (j + 1), GROUP * (j + 2), relay_block, 0)
        inner(0, j)
        give_back(j)
        arrive(j)
        inner(1, j)
        turn(every)
        for n in range(3):
            add(n, every)
        return 0

    lax.fori_loop(0, 3, superstep, 0)

    def core_copy(n):
        return pltpu.make_async_remote_copy(
            src_ref=work.at[n, pl.ds(0, LINES)],
            dst_ref=take.at[n],
            send_sem=core_send.at[n],
            recv_sem=core_recv.at[n],
            device_id=over_core,
            device_id_type=MESH,
        )

    inner(0, 3)
    give_back(3)
    turn(slice(0, ROWS))
    for n in range(3):
        add(n, slice(0, ROWS))
    arrive(3)
    late = slice(ROWS, 2 * ROWS)
    inner(1, 3)
    turn(late)
    other = pl.ds(pl.multiple_of((1 - c) * SHARD, 8), SHARD)
    mine = pl.ds(pl.multiple_of(c * SHARD, 8), SHARD)
    for n in range(3):
        add(n, late)
        work[n, 0:SHARD, 0:WIDTH] = acc[n, other, 0:WIDTH].astype(BF16)
        core_copy(n).start()
    for n in range(3):
        core_copy(n).wait_recv()
        total = (acc[n, mine, 0:WIDTH] + take[n, 0:SHARD, 0:WIDTH].astype(F32)).astype(BF16)
        if n < 2:
            out_gu_ref[:, n * WIDTH : (n + 1) * WIDTH] = total
        else:
            out_dn_ref[...] = total

    for n in range(3):
        core_copy(n).wait_send()

    def settle_block(r, _):
        forward_block(r).wait_send()
        return 0

    lax.fori_loop(1, OWNERS, settle_block, 0)
    some = back_ref.at[pl.ds(1, OWNERS - 1)]
    pltpu.make_async_copy(some, some, back_send).wait()
    pltpu.make_async_copy(some, some, back_recv).wait()
    own_back.wait()


def shards(tokens, d_out, route_ids, route_probs, w_gate_up, gate_up_bias, w_down):
    toks = tokens.shape[0]
    vmem = pl.BlockSpec(memory_space=pltpu.VMEM)
    hbm = pl.BlockSpec(memory_space=pl.ANY)
    slots = OWNERS * CAP
    block = (CAP, 2 * WIDTH)
    grads = (
        jax.ShapeDtypeStruct((SHARD, 2 * WIDTH), BF16),
        jax.ShapeDtypeStruct((SHARD, WIDTH), BF16),
    )
    pick, grad_gu, grad_dn, back = pl.pallas_call(
        main_kernel,
        name="experts",
        out_shape=(
            jax.ShapeDtypeStruct((slots, toks), BF16),
            *grads,
            jax.ShapeDtypeStruct((OWNERS, CAP, PAD), BF16),
        ),
        in_specs=[vmem] * 3 + [hbm] * 4,
        out_specs=(vmem, vmem, vmem, hbm),
        scratch_shapes=[
            pltpu.VMEM((WIDTH, toks), BF16),
            pltpu.VMEM((WIDTH, toks), BF16),
            pltpu.VMEM((OWNERS, toks), F32),
            pltpu.VMEM((OWNERS, toks), F32),
            pltpu.VMEM((8, 4, *block), BF16),
            pltpu.VMEM((2, 8, 4, *block), BF16),
            pltpu.VMEM((2 * ROWS, WIDTH), BF16),
            pltpu.VMEM((2 * ROWS, WIDTH), BF16),
            pltpu.VMEM((WIDTH, 2 * WIDTH), BF16),
            pltpu.VMEM((WIDTH, PAD), BF16),
            pltpu.VMEM((PAD, WIDTH), BF16),
            pltpu.VMEM((3, HALF, PAD), F32),
            pltpu.VMEM((3, 2 * ROWS, PAD), BF16),
            pltpu.VMEM((HALF, 2 * ROWS), BF16),
            pltpu.VMEM((HALF, 2 * ROWS), BF16),
            pltpu.VMEM((3, LINES, PAD), BF16),
            pltpu.SemaphoreType.DMA((4,)),
            pltpu.SemaphoreType.DMA((8,)),
            pltpu.SemaphoreType.DMA((OWNERS,)),
            pltpu.SemaphoreType.DMA((OWNERS,)),
            pltpu.SemaphoreType.DMA((OWNERS,)),
            pltpu.SemaphoreType.DMA,
            pltpu.SemaphoreType.DMA,
            pltpu.SemaphoreType.DMA,
            pltpu.SemaphoreType.DMA((3,)),
            pltpu.SemaphoreType.DMA((3,)),
        ],
        compiler_params=pltpu.CompilerParams(
            collective_id=0, has_side_effects=True, vmem_limit_bytes=63 * 2**20
        ),
    )(route_ids.T, route_probs.T, gate_up_bias, tokens.T, d_out.T, w_gate_up, w_down)
    d_tokens, grad_gu, grad_dn = pl.pallas_call(
        finish_kernel,
        name="finish",
        out_shape=(jax.ShapeDtypeStruct((WIDTH, toks), BF16), *grads),
        in_specs=[hbm] * 4,
        out_specs=(vmem, hbm, hbm),
        scratch_shapes=[
            pltpu.VMEM((slots, toks), BF16),
            pltpu.VMEM((slots, PAD), BF16),
            pltpu.VMEM((SHARD, 2 * WIDTH), BF16),
            pltpu.VMEM((SHARD, WIDTH), BF16),
            pltpu.SemaphoreType.DMA((6,)),
        ],
        compiler_params=pltpu.CompilerParams(vmem_limit_bytes=60 * 2**20),
    )(pick, back.reshape(slots, PAD), grad_gu, grad_dn)
    return d_tokens.T, grad_gu[None], grad_dn[None]


def solution(mesh):
    in_specs = (
        P(("dp", "expert"), None),
        P(("dp", "expert"), None),
        P(("dp", "expert"), None),
        P(("dp", "expert"), None),
        P("expert", None, None),
        P("expert", None),
        P("expert", None, None),
    )
    out_specs = (P(("dp", "expert"), None), P("expert", "dp", None), P("expert", "dp", None))
    return jax.shard_map(shards, mesh=mesh, in_specs=in_specs, out_specs=out_specs, check_vma=False)
```

time: 155 us -> 137 us (0.88)
  the two profiles are of different devices: /device:TPU:13 before, /device:TPU:47 now
where the time goes in v2:
time: 137 us
  Pallas kernels  136 us (99%)
    pallas_call x1, Pallas kernels, shards(): pl.pallas_call(main_kernel, name='experts', out_shape=(jax.ShapeDtypeStru...  131 us
    pallas_call x1, Pallas kernels, shards(): pl.pallas_call(finish_kernel, name='finish', out_shape=(jax.ShapeDtypeStr...  5.01 us

profile of v2, /device:TPU:47, one launch (start us, length us, event | category | flops | bytes accessed | tf_op | source)
XLA Modules:
  0.0 137.2 jit_solution(13101876606013116918)
XLA Ops:
  0.6 131.3 %experts.1 = (bf16[768,256]{1,0:T(8,128)(2,1)}, bf16[360,2880]{1,0:T(8,128)(2,1)}, bf16[360,1440]{1,0:T(8,128)(2,1)}, bf16[32,24,1536]{2,1,0:T(8,128)(2,1)}) custom-call(s32[4,256]{1,0:T(4,128)} %bitcast.11, f32[4,256]{1,0:T(4,128)} %bitcast.12, f32[1,2880]{1,0:T(1,128)} %bias_ref.1, bf16[1440,256]{1,0:T(8,128)(2,1)} %bitcast.9, bf16[1440,256]{1,0:T(8,128)(2,1)} %bitcast.10, ...), custom_call_target="tpu_custom_call" | custom-call | tf_op jit(solution)/shard_map/experts/pallas_call | solution.py:424
  132.0 5.0 %finish.1 = (bf16[1440,256]{1,0:T(8,128)(2,1)}, bf16[360,2880]{1,0:T(8,128)(2,1)}, bf16[360,1440]{1,0:T(8,128)(2,1)}) custom-call(bf16[768,256]{1,0:T(8,128)(2,1)} %get-tuple-element.10.pick_ref, bf16[768,1536]{1,0:T(8,128)(2,1)} %bitcast.8, bf16[360,2880]{1,0:T(8,128)(2,1)} %get-tuple-element.12.gu_ref, bf16[360,1440]{1,0:T(8,128)(2,1)} %get-tuple-element.13.dn_ref), custom_call_target="tpu_custom_call" | custom-call | tf_op jit(solution)/shard_map/finish/pallas_call | solution.py:466

commit v3 on v2

--- a/solution.py
+++ b/solution.py
@@ -17,6 +17,7 @@
 LINES = 368
 PAD = 1536
 TILE = 512
+PAGE = 256
 GROUP = 8
 ROWS = GROUP * CAP
 
@@ -34,26 +35,21 @@
 
 
 def finish_kernel(
-    pick_ref, back_ref, gu_ref, dn_ref, tok_ref, out_gu_ref, out_dn_ref, pick, back, gu, dn, sem
+    tok_ref, gu_ref, dn_ref, out_tok_ref, out_gu_ref, out_dn_ref, tok, gu, dn, sem
 ):
-    ins = [
-        pltpu.make_async_copy(src, dst, sem.at[n])
-        for n, (src, dst) in enumerate(
-            ((back_ref, back), (pick_ref, pick), (dn_ref, dn), (gu_ref, gu))
-        )
-    ]
-    outs = [
-        pltpu.make_async_copy(dn, out_dn_ref, sem.at[4]),
-        pltpu.make_async_copy(gu, out_gu_ref, sem.at[5]),
-    ]
+    parts = (
+        (gu_ref.at[:, 0:MAIN], gu.at[:, 0:MAIN], out_gu_ref.at[:, 0:MAIN]),
+        (gu_ref.at[:, MAIN:], gu.at[:, MAIN:], out_gu_ref.at[:, MAIN:]),
+        (dn_ref, dn, out_dn_ref),
+        (tok_ref, tok, out_tok_ref),
+    )
+    ins = [pltpu.make_async_copy(a, b, sem.at[0, n]) for n, (a, b, _) in enumerate(parts)]
+    outs = [pltpu.make_async_copy(b, c, sem.at[1, n]) for n, (_, b, c) in enumerate(parts)]
     for copy in ins:
         copy.start()
-    for n in range(2):
-        ins[2 + n].wait()
-        outs[n].start()
-    ins[0].wait()
-    ins[1].wait()
-    tok_ref[...] = tn(pick[...], back[:, 0:WIDTH]).astype(BF16).T
+    for first, second in zip(ins, outs):
+        first.wait()
+        second.start()
     for copy in outs:
         copy.wait()
 
@@ -66,10 +62,14 @@
     dout_ref,
     wgu_ref,
     wdn_ref,
-    pick_ref,
+    out_tok_ref,
     out_gu_ref,
     out_dn_ref,
     back_ref,
+    pick,
+    page,
+    out_gu,
+    out_dn,
     tok,
     dout,
     code,
@@ -85,6 +85,7 @@
     work,
     rows_t,
     hid_t,
+    give,
     take,
     load_sem,
     send_sem,
@@ -96,6 +97,8 @@
     self_sem,
     core_send,
     core_recv,
+    page_sem,
+    out_sem,
 ):
     dp = lax.axis_index("dp")
     me = lax.axis_index("expert")
@@ -167,7 +170,7 @@
         ones = jnp.where(chosen, 1.0, 0.0).reshape(ROWS, toks).astype(BF16)
         share = jnp.where(chosen, jnp.broadcast_to(prob[part, :][:, None, :], place.shape), 0.0)
         share = jnp.sum(share, axis=2, keepdims=True).reshape(ROWS, 1)
-        pick_ref[pl.ds(pl.multiple_of(g * ROWS, ROWS), ROWS), :] = ones
+        pick[pl.ds(pl.multiple_of(g * ROWS, ROWS), ROWS), :] = ones
         both = pl.ds(2 * g, 2)
         for n, src in enumerate((tok, dout)):
             value = nt(ones, src[...])
@@ -245,16 +248,17 @@
     lax.fori_loop(1, GROUP, relay_block, 0)
     acc[...] = jnp.zeros_like(acc)
 
-    def inner(region, j):
-        lines = slice(region * ROWS, (region + 1) * ROWS)
-        both = pl.ds(2 * j, 2)
+    def inner(region, first, count, start):
+        size = count * (GROUP // 2) * CAP
+        lines = slice(start, start + size)
+        both = pl.ds(first, count)
         tail = 2 * MAIN
         more = WIDTH - MAIN
         for n, dst in enumerate((rows, scaled)):
             dst[lines, 0:MAIN] = got[region, both, :, :, n * MAIN : (n + 1) * MAIN].reshape(
-                ROWS, MAIN
+                size, MAIN
             )
-        ends = got[region, both, :, :, tail : tail + 2 * more].reshape(ROWS, 2 * more)
+        ends = got[region, both, :, :, tail : tail + 2 * more].reshape(size, 2 * more)
         rows[lines, MAIN:WIDTH] = ends[:, 0:more]
         scaled[lines, MAIN:WIDTH] = ends[:, more:]
         for t in range(PAD // TILE):
@@ -322,12 +326,12 @@
 
         lax.fori_loop(GROUP * j, GROUP * j + GROUP, send_back, 0)
 
-    def arrive(j):
+    def arrive(first, count):
         def one(r, _):
             forward_block(r).wait_recv()
             return 0
 
-        lax.fori_loop(GROUP * j, GROUP * j + GROUP, one, 0)
+        lax.fori_loop(first, first + count, one, 0)
 
     def turn(lines):
         at = slice(0, lines.stop - lines.start)
@@ -335,38 +339,80 @@
 
             @pl.when(l == side)
             def _():
-                cols = slice(HALF * side, HALF * (side + 1))
-                rows_t[:, at] = rows[lines, cols].T
-                hid_t[:, at] = work[2, lines, cols].T
-
-    def add(n, lines):
-        left = (rows_t, rows_t, hid_t)[n].at[:, 0 : lines.stop - lines.start]
-        for t in range(PAD // TILE):
-            cols = slice(t * TILE, (t + 1) * TILE)
-            if n < 2:
-                acc[n, :, cols] += nn(left[...], work[n, lines, cols])
-            else:
-                cols = slice(t * TILE, min((t + 1) * TILE, WIDTH))
-                acc[n, :, cols] += nn(left[...], scaled[lines, cols])
+                for q in range(2):
+                    cols = slice(HALF * side + SHARD * q, HALF * side + SHARD * (q + 1))
+                    rows_t[q, :, at] = rows[lines, cols].T
+                    hid_t[q, :, at] = work[2, lines, cols].T
+
+    def product(n, q, t, lines):
+        left = (rows_t, rows_t, hid_t)[n][q, :, 0 : lines.stop - lines.start]
+        cols = slice(t * TILE, (t + 1) * TILE)
+        if n < 2:
+            return cols, nn(left, work[n, lines, cols])
+        cols = slice(t * TILE, min((t + 1) * TILE, WIDTH))
+        return cols, nn(left, scaled[lines, cols])
+
+    def add(lines):
+        for n in range(3):
+            for t in range(PAD // TILE):
+                for q in range(2):
+                    cols, value = product(n, q, t, lines)
+                    acc[n, q, :, cols] += value
 
     every = slice(0, 2 * ROWS)
 
+    def relay_group(g):
+        lax.fori_loop(GROUP * g, GROUP * (g + 1), relay_block, 0)
+
+    first = slice(0, ROWS)
+    inner(0, 0, 2, 0)
+    relay_group(1)
+    give_back(0)
+    turn(first)
+    add(first)
+
     def superstep(j, _):
-        lax.fori_loop(GROUP * (j + 1), GROUP * (j + 2), relay_block, 0)
-        inner(0, j)
-        give_back(j)
-        arrive(j)
-        inner(1, j)
+        @pl.when(j < 2)
+        def _():
+            relay_group(j + 2)
+
+        inner(0, 2 * j + 2, 2, 0)
+        give_back(j + 1)
+        arrive(GROUP * j, GROUP)
+        inner(1, 2 * j, 2, ROWS)
         turn(every)
-        for n in range(3):
-            add(n, every)
+        add(every)
         return 0
 
     lax.fori_loop(0, 3, superstep, 0)
+
+    def outgoing(n):
+        return give.at[n] if n < 2 else work.at[2, pl.ds(0, LINES)]
+
+    def turn_page(t):
+        cols = pl.ds(t * PAGE, PAGE)
+        return pltpu.make_async_copy(back_ref.at[:, :, cols], page.at[t % 2], page_sem.at[t % 2])
+
+    tok_out = pltpu.make_async_copy(tok, out_tok_ref, out_sem.at[3])
+
+    def combine():
+        some = back_ref.at[pl.ds(1, OWNERS - 1)]
+        pltpu.make_async_copy(some, some, back_recv).wait()
+        own_back.wait()
+        turn_page(0).start()
+        chosen = pick[...].T
+        for t in range(PAD // PAGE):
+            if t + 1 < PAD // PAGE:
+                turn_page(t + 1).start()
+            turn_page(t).wait()
+            value = nn(chosen, page[t % 2].reshape(OWNERS * CAP, PAGE)).astype(BF16).T
+            lines = slice(t * PAGE, min((t + 1) * PAGE, WIDTH))
+            tok[lines, :] = value[0 : lines.stop - lines.start]
+        tok_out.start()
 
     def core_copy(n):
         return pltpu.make_async_remote_copy(
-            src_ref=work.at[n, pl.ds(0, LINES)],
+            src_ref=outgoing(n),
             dst_ref=take.at[n],
             send_sem=core_send.at[n],
             recv_sem=core_recv.at[n],
@@ -374,28 +420,37 @@
             device_id_type=MESH,
         )
 
-    inner(0, 3)
-    give_back(3)
-    turn(slice(0, ROWS))
+    late = slice(ROWS, 2 * ROWS)
+    arrive(24, 4)
+    inner(1, 6, 1, ROWS)
+    arrive(28, 4)
+    inner(1, 7, 1, ROWS + ROWS // 2)
+    turn(late)
     for n in range(3):
-        add(n, slice(0, ROWS))
-    arrive(3)
-    late = slice(ROWS, 2 * ROWS)
-    inner(1, 3)
-    turn(late)
-    other = pl.ds(pl.multiple_of((1 - c) * SHARD, 8), SHARD)
-    mine = pl.ds(pl.multiple_of(c * SHARD, 8), SHARD)
-    for n in range(3):
-        add(n, late)
-        work[n, 0:SHARD, 0:WIDTH] = acc[n, other, 0:WIDTH].astype(BF16)
+        for t in range(PAD // TILE):
+            cols, value = product(n, 1 - c, t, late)
+            outgoing(n)[0:SHARD, cols] = (acc[n, 1 - c, :, cols] + value).astype(BF16)
         core_copy(n).start()
+    combine()
+    out_copies = (
+        pltpu.make_async_copy(
+            out_gu.at[:, 0:MAIN], out_gu_ref.at[:, 0:MAIN], out_sem.at[0]
+        ),
+        pltpu.make_async_copy(out_gu.at[:, MAIN:], out_gu_ref.at[:, MAIN:], out_sem.at[1]),
+        pltpu.make_async_copy(out_dn, out_dn_ref, out_sem.at[2]),
+    )
     for n in range(3):
         core_copy(n).wait_recv()
-        total = (acc[n, mine, 0:WIDTH] + take[n, 0:SHARD, 0:WIDTH].astype(F32)).astype(BF16)
-        if n < 2:
-            out_gu_ref[:, n * WIDTH : (n + 1) * WIDTH] = total
-        else:
-            out_dn_ref[...] = total
+        for t in range(PAD // TILE):
+            cols, value = product(n, c, t, late)
+            cols = slice(cols.start, min(cols.stop, WIDTH))
+            value = value[:, 0 : cols.stop - cols.start]
+            total = acc[n, c, :, cols] + value + take[n, 0:SHARD, cols].astype(F32)
+            if n < 2:
+                out_gu[:, n * WIDTH + cols.start : n * WIDTH + cols.stop] = total.astype(BF16)
+            else:
+                out_dn[:, cols] = total.astype(BF16)
+        out_copies[n].start()
 
     for n in range(3):
         core_copy(n).wait_send()
@@ -407,8 +462,8 @@
     lax.fori_loop(1, OWNERS, settle_block, 0)
     some = back_ref.at[pl.ds(1, OWNERS - 1)]
     pltpu.make_async_copy(some, some, back_send).wait()
-    pltpu.make_async_copy(some, some, back_recv).wait()
-    own_back.wait()
+    for copy in (*out_copies, tok_out):
+        copy.wait()
 
 
 def shards(tokens, d_out, route_ids, route_probs, w_gate_up, gate_up_bias, w_down):
@@ -417,21 +472,22 @@
     hbm = pl.BlockSpec(memory_space=pl.ANY)
     slots = OWNERS * CAP
     block = (CAP, 2 * WIDTH)
-    grads = (
+    results = (
+        jax.ShapeDtypeStruct((WIDTH, toks), BF16),
         jax.ShapeDtypeStruct((SHARD, 2 * WIDTH), BF16),
         jax.ShapeDtypeStruct((SHARD, WIDTH), BF16),
     )
-    pick, grad_gu, grad_dn, back = pl.pallas_call(
+    d_tokens, grad_gu, grad_dn, _ = pl.pallas_call(
         main_kernel,
         name="experts",
-        out_shape=(
-            jax.ShapeDtypeStruct((slots, toks), BF16),
-            *grads,
-            jax.ShapeDtypeStruct((OWNERS, CAP, PAD), BF16),
-        ),
+        out_shape=(*results, jax.ShapeDtypeStruct((OWNERS, CAP, PAD), BF16)),
         in_specs=[vmem] * 3 + [hbm] * 4,
-        out_specs=(vmem, vmem, vmem, hbm),
+        out_specs=(hbm, hbm, hbm, hbm),
         scratch_shapes=[
+            pltpu.VMEM((slots, toks), BF16),
+            pltpu.VMEM((2, OWNERS, CAP, PAGE), BF16),
+            pltpu.VMEM((SHARD, 2 * WIDTH), BF16),
+            pltpu.VMEM((SHARD, WIDTH), BF16),
             pltpu.VMEM((WIDTH, toks), BF16),
             pltpu.VMEM((WIDTH, toks), BF16),
             pltpu.VMEM((OWNERS, toks), F32),
@@ -443,10 +499,11 @@
             pltpu.VMEM((WIDTH, 2 * WIDTH), BF16),
             pltpu.VMEM((WIDTH, PAD), BF16),
             pltpu.VMEM((PAD, WIDTH), BF16),
-            pltpu.VMEM((3, HALF, PAD), F32),
+            pltpu.VMEM((3, 2, SHARD, PAD), F32),
             pltpu.VMEM((3, 2 * ROWS, PAD), BF16),
-            pltpu.VMEM((HALF, 2 * ROWS), BF16),
-            pltpu.VMEM((HALF, 2 * ROWS), BF16),
+            pltpu.VMEM((2, SHARD, 2 * ROWS), BF16),
+            pltpu.VMEM((2, SHARD, 2 * ROWS), BF16),
+            pltpu.VMEM((2, LINES, PAD), BF16),
             pltpu.VMEM((3, LINES, PAD), BF16),
             pltpu.SemaphoreType.DMA((4,)),
             pltpu.SemaphoreType.DMA((8,)),
@@ -458,26 +515,25 @@
             pltpu.SemaphoreType.DMA,
             pltpu.SemaphoreType.DMA((3,)),
             pltpu.SemaphoreType.DMA((3,)),
+            pltpu.SemaphoreType.DMA((2,)),
+            pltpu.SemaphoreType.DMA((4,)),
         ],
         compiler_params=pltpu.CompilerParams(
-            collective_id=0, has_side_effects=True, vmem_limit_bytes=63 * 2**20
+            collective_id=0, has_side_effects=True, vmem_limit_bytes=638 * 2**20 // 10
         ),
     )(route_ids.T, route_probs.T, gate_up_bias, tokens.T, d_out.T, w_gate_up, w_down)
     d_tokens, grad_gu, grad_dn = pl.pallas_call(
         finish_kernel,
         name="finish",
-        out_shape=(jax.ShapeDtypeStruct((WIDTH, toks), BF16), *grads),
-        in_specs=[hbm] * 4,
-        out_specs=(vmem, hbm, hbm),
+        out_shape=results,
+        in_specs=[hbm] * 3,
+        out_specs=(hbm, hbm, hbm),
         scratch_shapes=[
-            pltpu.VMEM((slots, toks), BF16),
-            pltpu.VMEM((slots, PAD), BF16),
-            pltpu.VMEM((SHARD, 2 * WIDTH), BF16),
-            pltpu.VMEM((SHARD, WIDTH), BF16),
-            pltpu.SemaphoreType.DMA((6,)),
+            *(pltpu.VMEM(result.shape, BF16) for result in results),
+            pltpu.SemaphoreType.DMA((2, 4)),
         ],
         compiler_params=pltpu.CompilerParams(vmem_limit_bytes=60 * 2**20),
-    )(pick, back.reshape(slots, PAD), grad_gu, grad_dn)
+    )(d_tokens, grad_gu, grad_dn)
     return d_tokens.T, grad_gu[None], grad_dn[None]
 
 

time: 137 us -> 133 us (0.971)
  Pallas kernels: 136 us -> 132 us
    pallas_call x2, Pallas kernels: 136 us -> 132 us  [the longest x1 129 us: shards(): pl.pallas_call(main_kernel, name='experts', out_shape=(*results, jax.Shap...]
where the time goes in v3:
time: 133 us
  Pallas kernels  132 us (99%)
    pallas_call x1, Pallas kernels, shards(): pl.pallas_call(main_kernel, name='experts', out_shape=(*results, jax.Shap...  129 us
    pallas_call x1, Pallas kernels, shards(): pl.pallas_call(finish_kernel, name='finish', out_shape=results, in_specs=...  3.22 us

profile of v3, /device:TPU:47, one launch (start us, length us, event | category | flops | bytes accessed | tf_op | source)
XLA Modules:
  0.0 133.1 jit_solution(11678295200836354201)
XLA Ops:
  0.6 129.1 %experts.1 = (bf16[1440,256]{1,0:T(8,128)(2,1)}, bf16[360,2880]{1,0:T(8,128)(2,1)}, bf16[360,1440]{1,0:T(8,128)(2,1)}, bf16[32,24,1536]{2,1,0:T(8,128)(2,1)}) custom-call(s32[4,256]{1,0:T(4,128)} %bitcast.9, f32[4,256]{1,0:T(4,128)} %bitcast.10, f32[1,2880]{1,0:T(1,128)} %bias_ref.1, bf16[1440,256]{1,0:T(8,128)(2,1)} %bitcast.7, bf16[1440,256]{1,0:T(8,128)(2,1)} %bitcast.8, ...), custom_call_target="tpu_custom_call" | custom-call | tf_op jit(solution)/shard_map/experts/pallas_call | solution.py:480
  129.7 3.2 %finish.1 = (bf16[1440,256]{1,0:T(8,128)(2,1)}, bf16[360,2880]{1,0:T(8,128)(2,1)}, bf16[360,1440]{1,0:T(8,128)(2,1)}) custom-call(bf16[1440,256]{1,0:T(8,128)(2,1)} %get-tuple-element.9.tok_ref, bf16[360,2880]{1,0:T(8,128)(2,1)} %get-tuple-element.10.gu_ref, bf16[360,1440]{1,0:T(8,128)(2,1)} %get-tuple-element.11.dn_ref), custom_call_target="tpu_custom_call" | custom-call | tf_op jit(solution)/shard_map/finish/pallas_call | solution.py:525

commit v4 on v3

--- a/solution.py
+++ b/solution.py
@@ -17,7 +17,6 @@
 LINES = 368
 PAD = 1536
 TILE = 512
-PAGE = 256
 GROUP = 8
 ROWS = GROUP * CAP
 
@@ -67,7 +66,6 @@
     out_dn_ref,
     back_ref,
     pick,
-    page,
     out_gu,
     out_dn,
     tok,
@@ -217,12 +215,21 @@
     relay_copy(send.at[0, 0], slot(1, 0), 0, over_y).start()
     lax.fori_loop(1, GROUP, dispatch, 0)
 
+    def landed(r):
+        pltpu.make_async_copy(slot(0, r), slot(0, r), recv_sem.at[r]).wait()
+
+    def relay_block(r, _):
+        landed(r)
+        forward_block(r).start()
+        return 0
+
     def fill_next(g, _):
         fill(g)
         lax.fori_loop(GROUP * g, GROUP * g + GROUP, dispatch, 0)
-        return 0
+        return relay_block(g, 0)
 
     lax.fori_loop(1, OWNERS // GROUP, fill_next, 0)
+    lax.fori_loop(OWNERS // GROUP, GROUP - 2, relay_block, 0)
 
     loads[2].wait()
     loads[3].wait()
@@ -237,15 +244,7 @@
     lax.fori_loop(0, 10, shift, 0)
     own.wait()
 
-    def landed(r):
-        pltpu.make_async_copy(slot(0, r), slot(0, r), recv_sem.at[r]).wait()
-
-    def relay_block(r, _):
-        landed(r)
-        forward_block(r).start()
-        return 0
-
-    lax.fori_loop(1, GROUP, relay_block, 0)
+    lax.fori_loop(GROUP - 2, GROUP, relay_block, 0)
     acc[...] = jnp.zeros_like(acc)
 
     def inner(region, first, count, start):
@@ -389,25 +388,29 @@
     def outgoing(n):
         return give.at[n] if n < 2 else work.at[2, pl.ds(0, LINES)]
 
-    def turn_page(t):
-        cols = pl.ds(t * PAGE, PAGE)
-        return pltpu.make_async_copy(back_ref.at[:, :, cols], page.at[t % 2], page_sem.at[t % 2])
+    def returned(p):
+        return pltpu.make_async_copy(
+            back_ref.at[pl.ds(4 * p, 4)], got.at[0, p, :, :, pl.ds(0, PAD)], page_sem.at[p]
+        )
+
+    def fetch(p, _):
+        returned(p).start()
+        return 0
+
+    def settle(r, _):
+        forward_block(r).wait_send()
+        return 0
 
     tok_out = pltpu.make_async_copy(tok, out_tok_ref, out_sem.at[3])
 
     def combine():
-        some = back_ref.at[pl.ds(1, OWNERS - 1)]
-        pltpu.make_async_copy(some, some, back_recv).wait()
-        own_back.wait()
-        turn_page(0).start()
+        for p in range(8):
+            returned(p).wait()
         chosen = pick[...].T
-        for t in range(PAD // PAGE):
-            if t + 1 < PAD // PAGE:
-                turn_page(t + 1).start()
-            turn_page(t).wait()
-            value = nn(chosen, page[t % 2].reshape(OWNERS * CAP, PAGE)).astype(BF16).T
-            lines = slice(t * PAGE, min((t + 1) * PAGE, WIDTH))
-            tok[lines, :] = value[0 : lines.stop - lines.start]
+        for t in range(PAD // TILE):
+            cols = slice(t * TILE, min((t + 1) * TILE, WIDTH))
+            page = got[0, :, :, :, cols].reshape(OWNERS * CAP, cols.stop - cols.start)
+            tok[cols, :] = nn(chosen, page).astype(BF16).T
         tok_out.start()
 
     def core_copy(n):
@@ -425,6 +428,11 @@
     inner(1, 6, 1, ROWS)
     arrive(28, 4)
     inner(1, 7, 1, ROWS + ROWS // 2)
+    lax.fori_loop(1, OWNERS, settle, 0)
+    some = back_ref.at[pl.ds(1, OWNERS - 1)]
+    pltpu.make_async_copy(some, some, back_recv).wait()
+    own_back.wait()
+    lax.fori_loop(0, 8, fetch, 0)
     turn(late)
     for n in range(3):
         for t in range(PAD // TILE):
@@ -455,11 +463,6 @@
     for n in range(3):
         core_copy(n).wait_send()
 
-    def settle_block(r, _):
-        forward_block(r).wait_send()
-        return 0
-
-    lax.fori_loop(1, OWNERS, settle_block, 0)
     some = back_ref.at[pl.ds(1, OWNERS - 1)]
     pltpu.make_async_copy(some, some, back_send).wait()
     for copy in (*out_copies, tok_out):
@@ -485,7 +488,6 @@
         out_specs=(hbm, hbm, hbm, hbm),
         scratch_shapes=[
             pltpu.VMEM((slots, toks), BF16),
-            pltpu.VMEM((2, OWNERS, CAP, PAGE), BF16),
             pltpu.VMEM((SHARD, 2 * WIDTH), BF16),
             pltpu.VMEM((SHARD, WIDTH), BF16),
             pltpu.VMEM((WIDTH, toks), BF16),
@@ -515,7 +517,7 @@
             pltpu.SemaphoreType.DMA,
             pltpu.SemaphoreType.DMA((3,)),
             pltpu.SemaphoreType.DMA((3,)),
-            pltpu.SemaphoreType.DMA((2,)),
+            pltpu.SemaphoreType.DMA((8,)),
             pltpu.SemaphoreType.DMA((4,)),
         ],
         compiler_params=pltpu.CompilerParams(

time: 133 us -> 149 us (1.12)
  the two profiles are of different devices: /device:TPU:47 before, /device:TPU:77 now
where the time goes in v4:
time: 149 us; the launch traced here: 148 us
  Pallas kernels  148 us (99%)
    pallas_call x1, Pallas kernels, shards(): pl.pallas_call(main_kernel, name='experts', out_shape=(*results, jax.Shap...  144 us
    pallas_call x1, Pallas kernels, shards(): pl.pallas_call(finish_kernel, name='finish', out_shape=results, in_specs=...  3.22 us

profile of v4, /device:TPU:77, one launch (start us, length us, event | category | flops | bytes accessed | tf_op | source)
XLA Modules:
  0.0 148.4 jit_solution(2092709609599520878)
XLA Ops:
  0.6 144.4 %experts.1 = (bf16[1440,256]{1,0:T(8,128)(2,1)}, bf16[360,2880]{1,0:T(8,128)(2,1)}, bf16[360,1440]{1,0:T(8,128)(2,1)}, bf16[32,24,1536]{2,1,0:T(8,128)(2,1)}) custom-call(s32[4,256]{1,0:T(4,128)} %bitcast.9, f32[4,256]{1,0:T(4,128)} %bitcast.10, f32[1,2880]{1,0:T(1,128)} %bias_ref.1, bf16[1440,256]{1,0:T(8,128)(2,1)} %bitcast.7, bf16[1440,256]{1,0:T(8,128)(2,1)} %bitcast.8, ...), custom_call_target="tpu_custom_call" | custom-call | tf_op jit(solution)/shard_map/experts/pallas_call | solution.py:483
  145.0 3.2 %finish.1 = (bf16[1440,256]{1,0:T(8,128)(2,1)}, bf16[360,2880]{1,0:T(8,128)(2,1)}, bf16[360,1440]{1,0:T(8,128)(2,1)}) custom-call(bf16[1440,256]{1,0:T(8,128)(2,1)} %get-tuple-element.9.tok_ref, bf16[360,2880]{1,0:T(8,128)(2,1)} %get-tuple-element.10.gu_ref, bf16[360,1440]{1,0:T(8,128)(2,1)} %get-tuple-element.11.dn_ref), custom_call_target="tpu_custom_call" | custom-call | tf_op jit(solution)/shard_map/finish/pallas_call | solution.py:527
